TPU v7x, 128 devices: a whole 4x4x4 slice. The times are simulated.
128 devices in a mesh: row: 4 (over z_hi, core), col: 32 (over z_lo, x, y).
Axes of the slice: x: 4, y: 4, z: 4 (z_hi: 2, z_lo: 2; z = z_hi * 2 + z_lo), core: 2. Of those that a mesh axis runs over, the one named last changes fastest.
Arguments:
- weight: bfloat16 [12288, 53248], P('row', 'col'), may hold values from -6 to 6
- sketch: bfloat16 [53248, 64], P('col'), may hold values from -6 to 6
- codebook: bfloat16 [16], replicated, may hold values from -1 to 1, as said below
Outputs:
- quant_weight: bfloat16 [12288, 53248], P(('row', 'col'))
- block_scales: float32 [12288, 832], P(('row', 'col'))
- lora_a: float32 [12288, 64], P('row')
- lora_b: float32 [64, 53248], P(None, 'col')
Inputs may be any that keep to these rules, and one draw needn't show every extreme that they name: `codebook`: strictly increasing, first entry -1 and last entry 1.
All inputs are finite; a program needn't handle non-finite values.
Results may differ from a plain program's by a relative error of at most 0.013.
Values may be sent and summed in bfloat16 or wider, within the bound.
A program may use at most 192 MiB of HBM per device.

v0:
```python
import math

import jax
import jax.numpy as jnp
from jax import lax
from jax.sharding import PartitionSpec as P

ROWS = 12288
BLOCK = 64
POWER = 2
LEVELS = 16


def quantize(block_rows, codebook):
    rows, cols = block_rows.shape
    values = block_rows.astype(jnp.float32)
    scales = jnp.max(jnp.abs(values.reshape(rows, cols // BLOCK, BLOCK)), axis=2)
    spread = jnp.repeat(scales, BLOCK, axis=1)
    levels = codebook.astype(jnp.float32)
    middles = (levels[:-1] + levels[1:]) * 0.5
    jumps = levels[1:] - levels[:-1]
    level = jnp.zeros_like(values) + levels[0]
    for index in range(LEVELS - 1):
        level = level + jnp.where(values > middles[index] * spread, jumps[index], 0.0)
    return (level * spread, scales)


def solve_basis(sample, gram):
    lower = jnp.linalg.cholesky(gram)
    return jax.scipy.linalg.solve_triangular(lower, sample.T, lower=True).T


def body(weight, sketch, codebook):
    high = lax.Precision.HIGHEST
    dequant, tile_scales = quantize(weight, codebook)
    residual = weight.astype(jnp.float32) - dequant
    quant_weight, block_scales = (
        lax.all_to_all(
            dequant.astype(jnp.bfloat16), "col", split_axis=0, concat_axis=1, tiled=True
        ),
        lax.all_to_all(
            tile_scales.astype(jnp.bfloat16), "col", split_axis=0, concat_axis=1, tiled=True
        ).astype(tile_scales.dtype),
    )

    def orthonormal(factor):
        partial_sample = jnp.dot(
            residual, factor, precision=high, preferred_element_type=jnp.float32
        )
        sample = lax.psum(partial_sample, "col")
        gram = lax.psum(
            jnp.dot(sample.T, sample, precision=high, preferred_element_type=jnp.float32), "row"
        )
        return solve_basis(sample, gram)

    def projection(basis):
        partial_project = jnp.dot(
            residual.T, basis, precision=high, preferred_element_type=jnp.float32
        )
        return lax.psum(partial_project, "row")

    basis = orthonormal(sketch.astype(jnp.float32))
    for step in range(POWER):
        basis = orthonormal(projection(basis))
    project = projection(basis)
    factor = math.sqrt(ROWS)
    return (quant_weight, block_scales, basis * factor, project.T / factor)


def solution(mesh):
    in_specs = (P("row", "col"), P("col", None), P())
    out_specs = (P(("row", "col"), None), P(("row", "col"), None), P("row", None), P(None, "col"))
    return jax.shard_map(body, mesh=mesh, in_specs=in_specs, out_specs=out_specs, check_vma=False)
```

profile of v0, /device:TPU:1, one launch (start us, length us, event | category | flops | bytes accessed | tf_op | source)
XLA Modules:
  0.0 1466.6 jit_solution(3520625236449382745)
XLA Ops:
  7.2 0.0 all-reduce.7.cloned.1.call-start
  7.2 0.7 convert_element_type.27
  7.9 1.1 slice.109
  9.1 0.1 add_multiply_fusion
  9.1 0.7 fusion.19
  9.8 0.7 fusion.20
  10.6 14.2 copy.45
  24.8 13.7 convert_abs_fusion
  38.5 8.8 reduce_max.9
  47.3 56.0 %convert_subtract_fusion = (f32[3072,1664]{0,1:T(8,128)}, bf16[3072,1664]{0,1:T(8,128)(2,1)}) fusion(bf16[3072,1664]{0,1:T(8,128)(2,1)} %copy.45, f32[]{:T(128)} %bitcast.32, f32[]{:T(128)} %bitcast.31, f32[]{:T(128)} %bitcast.30, f32[]{:T(128)} %bitcast.29, f32[]{:T(128)} %bitcast.28, f32[]{:T(128)} %bitcast.27, f32[]{:T(128)} %bitcast.26, f32[]{:T(128)} %bitcast.25, ...), kind=kLoop, calls=%fused_computation.16 | loop fusion | flops 327155712 | bytes 41214076 | tf_op jit(solution)/shard_map/sub | solution.py:36
  103.3 13.7 fusion.21
  117.0 0.0 all-reduce.7.cloned.1.call-update
  117.1 0.2 convert_element_type.31
  117.3 0.8 copy.48
  118.1 9.2 all-to-all-start.1
  127.3 14.0 copy.46
  141.3 265.2 %all-reduce.7.cloned.1.call-done = f32[3072,64]{0,1:T(8,128)} async-done(((f32[3072,64]{0,1:T(8,128)}), f32[3072,64]{0,1:T(8,128)}) %all-reduce.7.cloned.1.call-update) | async-done | bytes 786448 | tf_op jit(solution)/shard_map/psum | solution.py:50
  406.5 2.2 fusion.22
  408.6 36.1 %psum.64 = f32[64,64]{0,1:T(8,128)S(1)} all-reduce(f32[64,64]{0,1:T(8,128)S(1)} %fusion.22), channel_id=1, replica_groups=mesh['row'=4,'col'=32] {'row'}, use_global_device_ids=true, to_apply=%region_2.3 | all-reduce | flops 4096 | bytes 32768 | tf_op jit(solution)/shard_map/psum | solution.py:51
  444.7 0.1 copy.50
  444.8 5.8 cholesky.59
  450.7 0.6 compare_reduce_fusion.2
  451.3 0.7 fusion.6
  452.0 4.9 custom-call.7
  456.9 2.0 fusion.4
  458.9 7.0 all-to-all-start
  465.8 0.0 all-reduce.9.cloned.1.call-start
  465.9 23.6 %fusion.23 = f32[1664,64]{0,1:T(8,128)} fusion(f32[3072,1664]{0,1:T(8,128)} %get-tuple-element.22, f32[64,3072]{1,0:T(8,128)S(1)} %fusion.4), kind=kOutput, calls=%fused_computation.73 | convolution fusion | flops 3925868544 | bytes 21659648 | tf_op jit(solution)/shard_map/dot_general | solution.py:57
  489.5 0.2 all-reduce.11.cloned.1.call-start
  489.7 107.5 %all-reduce.9.cloned.1.call-done = f32[1664,64]{0,1:T(8,128)} async-done(((f32[1664,64]{0,1:T(8,128)}), f32[1664,64]{0,1:T(8,128)}) %all-reduce.9.cloned.1.call-update) | async-done | bytes 426000 | tf_op jit(solution)/shard_map/psum | solution.py:60
  597.3 17.9 %fusion.24 = f32[3072,64]{0,1:T(8,128)} fusion(f32[3072,1664]{0,1:T(8,128)} %get-tuple-element.22, f32[1664,64]{0,1:T(8,128)} %all-reduce.9.cloned.1.call-done), kind=kOutput, calls=%fused_computation.74 | convolution fusion | flops 3925868544 | bytes 21659648 | tf_op jit(solution)/shard_map/dot_general | solution.py:47
  615.2 0.0 all-reduce.11.cloned.1.call-update
  615.2 0.0 all-reduce.13.cloned.1.call-start
  615.3 294.1 %all-reduce.11.cloned.1.call-done = f32[3072,64]{0,1:T(8,128)} async-done(((f32[3072,64]{0,1:T(8,128)}), f32[3072,64]{0,1:T(8,128)}) %all-reduce.11.cloned.1.call-update) | async-done | bytes 786448 | tf_op jit(solution)/shard_map/psum | solution.py:50
  909.4 2.1 fusion.25
  911.5 35.8 %psum.67 = f32[64,64]{0,1:T(8,128)S(1)} all-reduce(f32[64,64]{0,1:T(8,128)S(1)} %fusion.25), channel_id=1, replica_groups=mesh['row'=4,'col'=32] {'row'}, use_global_device_ids=true, to_apply=%region_7.10 | all-reduce | flops 4096 | bytes 32768 | tf_op jit(solution)/shard_map/psum | solution.py:51
  947.3 0.1 copy.52
  947.4 5.8 cholesky.70
  953.3 0.6 compare_reduce_fusion.1
  953.9 0.7 fusion.7
  954.6 4.9 custom-call.8
  959.5 2.0 fusion.2
  961.5 23.6 %fusion.26 = f32[1664,64]{0,1:T(8,128)} fusion(f32[3072,1664]{0,1:T(8,128)} %get-tuple-element.22, f32[64,3072]{1,0:T(8,128)S(1)} %fusion.2), kind=kOutput, calls=%fused_computation.76 | convolution fusion | flops 3925868544 | bytes 21659648 | tf_op jit(solution)/shard_map/dot_general | solution.py:57
  985.1 0.3 all-reduce.15.cloned.1.call-start
  985.4 42.1 %all-reduce.13.cloned.1.call-done = f32[1664,64]{0,1:T(8,128)} async-done(((f32[1664,64]{0,1:T(8,128)}), f32[1664,64]{0,1:T(8,128)}) %all-reduce.13.cloned.1.call-update) | async-done | bytes 426000 | tf_op jit(solution)/shard_map/psum | solution.py:60
  1027.5 17.9 %fusion.27 = f32[3072,64]{0,1:T(8,128)} fusion(f32[3072,1664]{0,1:T(8,128)} %get-tuple-element.22, f32[1664,64]{0,1:T(8,128)} %all-reduce.13.cloned.1.call-done), kind=kOutput, calls=%fused_computation.77 | convolution fusion | flops 3925868544 | bytes 21659648 | tf_op jit(solution)/shard_map/dot_general | solution.py:47
  1045.4 0.0 all-reduce.15.cloned.1.call-update
  1045.5 0.0 all-reduce.17.cloned.1.call-start
  1045.5 0.1 convert_bitcast_fusion
  1045.6 0.9 copy.55
  1046.5 283.8 %all-reduce.15.cloned.1.call-done = f32[3072,64]{0,1:T(8,128)} async-done(((f32[3072,64]{0,1:T(8,128)}), f32[3072,64]{0,1:T(8,128)}) %all-reduce.15.cloned.1.call-update) | async-done | bytes 786448 | tf_op jit(solution)/shard_map/psum | solution.py:50
  1330.3 2.1 fusion.28
  1332.5 35.8 %psum.70 = f32[64,64]{0,1:T(8,128)S(1)} all-reduce(f32[64,64]{0,1:T(8,128)S(1)} %fusion.28), channel_id=1, replica_groups=mesh['row'=4,'col'=32] {'row'}, use_global_device_ids=true, to_apply=%region_10.13 | all-reduce | flops 4096 | bytes 32768 | tf_op jit(solution)/shard_map/psum | solution.py:51
  1368.3 0.1 copy.54
  1368.4 5.8 cholesky.81
  1374.3 0.6 compare_reduce_fusion
  1374.9 0.7 fusion.8
  1375.6 4.9 custom-call.9
  1380.5 2.0 fusion
  1382.5 23.6 %fusion.29 = f32[1664,64]{0,1:T(8,128)} fusion(f32[3072,1664]{0,1:T(8,128)} %get-tuple-element.22, f32[64,3072]{1,0:T(8,128)S(1)} %fusion), kind=kOutput, calls=%fused_computation.79 | convolution fusion | flops 3925868544 | bytes 21659648 | tf_op jit(solution)/shard_map/dot_general | solution.py:57
  1406.1 0.9 multiply_bitcast_fusion
  1407.1 41.4 %all-reduce.17.cloned.1.call-done = f32[1664,64]{0,1:T(8,128)} async-done(((f32[1664,64]{0,1:T(8,128)}), f32[1664,64]{0,1:T(8,128)}) %all-reduce.17.cloned.1.call-update) | async-done | bytes 426000 | tf_op jit(solution)/shard_map/psum | solution.py:60
  1448.5 1.8 multiply_bitcast_fusion.1
  1450.3 8.9 copy.59
  (17 shorter events, 0.3 us)
Async XLA Ops:
  7.2 96.2 %copy-start = (bf16[1664,64]{0,1:T(8,128)(2,1)S(1)}, bf16[1664,64]{0,1:T(8,128)(2,1)}, u32[]{:S(2)}) copy-start(bf16[1664,64]{0,1:T(8,128)(2,1)} %param.7) | copy-start | bytes 638980
  7.2 399.3 %all-reduce.7.cloned.1.call-start = ((), (), s32[]{:S(2)}) async-start(), calls=%async_computation.2 | async-start | bytes 1572864 | tf_op jit(solution)/shard_map/psum | solution.py:50
  118.1 340.8 %all-to-all-start.1 = ((bf16[32,96,26]{1,2,0:T(8,128)(2,1)}), bf16[32,96,26]{1,2,0:T(8,128)(2,1)S(1)}, u32[]{:S(2)}, u32[]{:S(2)}) async-start(bf16[32,96,26]{1,2,0:T(8,128)(2,1)} %copy.48), calls=%async_computation.1 | async-start | bytes 524288 | tf_op jit(solution)/shard_map/all_to_all | solution.py:41
  458.9 991.4 %all-to-all-start = ((bf16[32,96,1664]{2,1,0:T(8,128)(2,1)}), bf16[32,96,1664]{2,1,0:T(8,128)(2,1)}, u32[]{:S(2)}, u32[]{:S(2)}) async-start(bf16[32,96,1664]{2,1,0:T(8,128)(2,1)} %bitcast.179), calls=%async_computation | async-start | bytes 20447232 | tf_op jit(solution)/shard_map/all_to_all | solution.py:38
  465.8 131.4 %all-reduce.9.cloned.1.call-start = ((), (), s32[]{:S(2)}) async-start(), calls=%async_computation.3 | async-start | bytes 851968 | tf_op jit(solution)/shard_map/psum | solution.py:60
  489.5 419.9 %all-reduce.11.cloned.1.call-start = ((), (), s32[]{:S(2)}) async-start(), calls=%async_computation.4 | async-start | bytes 1572864 | tf_op jit(solution)/shard_map/psum | solution.py:50
  615.2 412.2 %all-reduce.13.cloned.1.call-start = ((), (), s32[]{:S(2)}) async-start(), calls=%async_computation.5 | async-start | bytes 851968 | tf_op jit(solution)/shard_map/psum | solution.py:60
  985.1 345.2 %all-reduce.15.cloned.1.call-start = ((), (), s32[]{:S(2)}) async-start(), calls=%async_computation.6 | async-start | bytes 1572864 | tf_op jit(solution)/shard_map/psum | solution.py:50
  1045.5 403.1 %all-reduce.17.cloned.1.call-start = ((), (), s32[]{:S(2)}) async-start(), calls=%async_computation.7 | async-start | bytes 851968 | tf_op jit(solution)/shard_map/psum | solution.py:60
  1380.5 78.8 %copy-start.1 = (bf16[1664,64]{0,1:T(8,128)(2,1)S(1)}, bf16[1664,64]{0,1:T(8,128)(2,1)}, u32[]{:S(2)}) copy-start(bf16[1664,64]{0,1:T(8,128)(2,1)} %param.7) | copy-start | bytes 638980
Sparse Core Ops, SparseCore 0:
  117.2 289.2 all-reduce.6
  489.6 107.5 all-reduce.8
  615.4 293.9 all-reduce.10
  985.2 42.2 all-reduce.12
  1045.6 284.6 all-reduce.14
  1406.2 42.2 all-reduce.16
where the time goes:
time: 1480 us; the launch traced here: 1470 us
  waiting for transfers between devices  1030 us (70%)
  matrix products  133 us (9%)
  other arithmetic  118 us (8%)
  blocking collectives  108 us (7%)
  local copies, waits for them, and re-layouts  41.9 us (3%)
  starting transfers between devices  16.9 us (1%)
  between operations  14.8 us (1%)
    psum x3, waiting for transfers between devices, orthonormal(): sample = lax.psum(partial_sample, 'col')  843 us
    psum x3, waiting for transfers between devices, projection(): return lax.psum(partial_project, 'row')  191 us
    psum x3, blocking collectives, orthonormal(): lax.psum(jnp.dot(sample.T, sample, precision=high, preferred_element_type...  108 us
    dot_general x3, matrix products, projection(): jnp.dot(residual.T, basis, precision=high, preferred_element_type=jnp.flo...  70.8 us
    sub x1, other arithmetic, body(): residual = weight.astype(jnp.float32) - dequant  56 us
    dot_general x3, matrix products, orthonormal(): jnp.dot(residual, factor, precision=high, preferred_element_type=jnp.floa...  49.6 us
  transfers between devices with their start and end apart: 8, of which 6 were waited for; matrix products, arithmetic and copies ran while one was open for 12% of the time, Pallas kernels for 0%

commit v1 on v0

v1 whole, which is shorter than its diff:
```python
import functools
import math

import jax
import jax.numpy as jnp
from jax import lax
from jax.experimental import pallas as pl
from jax.experimental.pallas import tpu as pltpu
from jax.sharding import PartitionSpec as P

ROWS = 12288
BLOCK = 64
POWER = 2
LEVELS = 16
RANK = 64
NCOL = 32
HIGH = lax.Precision.HIGHEST
MESH = pl.DeviceIdType.MESH
F32 = jnp.float32
BF16 = jnp.bfloat16

ROUNDS = (
    ((1, 1, 0), (3, 3, 1)),
    ((2, 0, 0), (0, 2, 1)),
    ((1, 3, 0), (3, 1, 1)),
    ((2, 1, 0), (0, 3, 1)),
    ((1, 2, 0), (3, 0, 1)),
    ((2, 2, 1),),
    ((1, 1, 1), (3, 3, 0)),
    ((2, 3, 0), (0, 1, 1)),
    ((3, 2, 0), (1, 0, 1)),
    ((2, 0, 1), (0, 2, 0)),
    ((1, 3, 1), (3, 1, 0)),
    ((2, 1, 1), (0, 3, 0)),
    ((1, 2, 1), (3, 0, 0)),
    ((2, 3, 1), (0, 1, 0)),
    ((3, 2, 1), (1, 0, 0)),
    ((2, 2, 0), (0, 0, 1)),
)
CODES = tuple(dx + 4 * dy + 16 * dz for group in ROUNDS for dx, dy, dz in group)
EARLY = 8
PACE = (2, 2, 2, 1, 1, 2, 2, 2, 1, 1, 2, 2, 1, 1, 1)


def partner(me, code):
    x, y, z = (me // 4) % 4, me % 4, me // 16
    dx, dy, dz = code % 4, (code // 4) % 4, code // 16
    return (z + dz) % 2 * 16 + (x + dx) % 4 * 4 + (y + dy) % 4


def code_at(index):
    code = 0
    for place, value in enumerate(CODES):
        code = jnp.where(index == place, value, code)
    return code


def dot(a, b, precision=None):
    return lax.dot_general(a, b, (((1,), (0,)), ((), ())), precision=precision, preferred_element_type=F32)


def dot_nt(a, b, precision=None):
    return lax.dot_general(a, b, (((1,), (1,)), ((), ())), precision=precision, preferred_element_type=F32)


def drain(ref, sem):
    pltpu.make_async_copy(ref, ref, sem).wait()


def kernel(
    weight, sketch, codebook,
    quant, scales, lora_a, lora_b,
    deq, res, scale_out, factor_top, factor_bot, sample_out, reduce_in, gather_in, sample_t,
    project, half_in, pair_in, total, gram_in, gram_out, work,
    load_sem, block_sem, scale_sem, own_sem, reduce_sem, gather_sem, half_sem, pair_sem, total_sem, gram_sem,
):
    cols = deq.shape[2]
    tiles = cols // 128
    per_block = deq.shape[1]
    half = per_block // 2
    row, me = lax.axis_index("row"), lax.axis_index("col")
    core = row % 2
    mate = row + 1 - 2 * core
    across = (row + 2) % 4
    peers = [partner(me, code) for code in CODES]

    def load(index):
        return pltpu.make_async_copy(
            weight.at[pl.ds(pl.multiple_of(index * per_block, per_block), per_block), :], deq.at[index], load_sem.at[index]
        )

    def start_load(index, carry):
        load(partner(me, code_at(index))).start()
        return carry

    lax.fori_loop(0, NCOL, start_load, 0)

    barrier = pltpu.get_barrier_semaphore()
    for peer in peers:
        pl.semaphore_signal(barrier, inc=1, device_id=(row, peer), device_id_type=MESH)
    for other in (1, 2, 3):
        pl.semaphore_signal(barrier, inc=1, device_id=((row + other) % 4, me), device_id_type=MESH)

    unit = (lax.broadcasted_iota(jnp.int32, (RANK, RANK), 0) == lax.broadcasted_iota(jnp.int32, (RANK, RANK), 1))
    factor_top[...] = jnp.zeros(factor_top.shape, BF16)
    factor_bot[...] = jnp.zeros(factor_bot.shape, BF16)
    turned = dot_nt(unit.astype(BF16), sketch[...]).astype(BF16)
    factor_top[0:RANK, :] = turned
    factor_bot[RANK : 2 * RANK, :] = turned

    levels = [codebook[k] for k in range(LEVELS)]
    middles = []
    for k in range(LEVELS - 1):
        middle = (levels[k] + levels[k + 1]) * 0.5
        middles.append(middle + jnp.abs(middle) * 2.0**-21)

    pl.semaphore_wait(barrier, len(peers) + 3)

    def send_block(place, peer):
        blocks = pltpu.make_async_remote_copy(
            src_ref=deq.at[peer], dst_ref=quant.at[:, pl.ds(pl.multiple_of(me * cols, 128), cols)],
            send_sem=block_sem.at[0], recv_sem=block_sem.at[1], device_id=(row, peer), device_id_type=MESH,
        )
        blocks.start()
        pltpu.make_async_remote_copy(
            src_ref=scale_out.at[peer], dst_ref=scales.at[me],
            send_sem=scale_sem.at[0], recv_sem=scale_sem.at[1], device_id=(row, peer), device_id_type=MESH,
        ).start()

    lane = lax.broadcasted_iota(jnp.int32, (16, 128), 1)

    def quantize_block(place, carry):
        block = partner(me, code_at(place))
        load(block).wait()

        def quantize_rows(group, inner):
            rows = pl.ds(pl.multiple_of(group * 16, 16), 16)
            shift = group // 2 * 32
            gathered = jnp.zeros((16, 128), F32)
            for tile in range(tiles):
                columns = slice(tile * 128, tile * 128 + 128)
                value = deq[block, rows, columns].astype(F32)
                size = jnp.abs(value)
                left = jnp.max(jnp.where(lane < BLOCK, size, 0.0), axis=1, keepdims=True)
                right = jnp.max(jnp.where(lane < BLOCK, 0.0, size), axis=1, keepdims=True)
                gathered = jnp.where(lane == shift + 2 * tile, left, gathered)
                gathered = jnp.where(lane == shift + 2 * tile + 1, right, gathered)
                spread = jnp.where(lane < BLOCK, left, right)
                unit_value = value * (1.0 / spread)
                level = jnp.full((16, 128), levels[0], F32)
                for k in range(LEVELS - 1):
                    level = jnp.where(unit_value > middles[k], levels[k + 1], level)
                dequant = level * spread
                deq[block, rows, columns] = dequant.astype(BF16)
                res[block, group // 3, pl.ds(pl.multiple_of(group % 3 * 16, 16), 16), columns] = (value - dequant).astype(BF16)
            held = pl.ds(pl.multiple_of(group % 2 * 16, 16), 16)
            before = scale_out[block, held, :].astype(F32)
            scale_out[block, held, :] = jnp.where(lane < shift, before, gathered).astype(BF16)
            return inner

        lax.fori_loop(0, per_block // 16, quantize_rows, 0)

        @pl.when(place < EARLY)
        def _():
            send_block(place, block)

        return carry

    scale_out[...] = jnp.zeros(scale_out.shape, BF16)
    lax.fori_loop(0, NCOL, quantize_block, 0)

    own = [
        pltpu.make_async_copy(deq.at[me], quant.at[:, pl.ds(pl.multiple_of(me * cols, 128), cols)], own_sem.at[0]),
        pltpu.make_async_copy(scale_out.at[me], scales.at[me], own_sem.at[1]),
    ]

    state = {"sent": EARLY, "point": 0}

    def breathe(last=False):
        count = len(CODES) if last else PACE[state["point"]]
        state["point"] += 1
        for place in range(state["sent"], min(state["sent"] + count, len(CODES))):
            send_block(place, peers[place])
            state["sent"] = place + 1

    def sample(step):
        def some(part, carry):
            blocks = pl.ds(pl.multiple_of(part * 8, 8), 8)
            top = res[blocks, 0].reshape(8 * half, cols)
            bottom = res[blocks, 1].reshape(8 * half, cols)
            both = dot_nt(top, factor_top[...]) + dot_nt(bottom, factor_bot[...])
            both = both[:, 0:128] + both[:, 128:256]
            sample_out[blocks] = both.reshape(8, half, 128).astype(BF16)
            return carry

        lax.fori_loop(0, NCOL // 8, some, 0)
        reduce_in[step, pl.ds(me, 1)] = sample_out[pl.ds(me, 1)]
        for peer in peers:
            pltpu.make_async_remote_copy(
                src_ref=sample_out.at[peer], dst_ref=reduce_in.at[step, me],
                send_sem=reduce_sem.at[step, 0], recv_sem=reduce_sem.at[step, 1], device_id=(row, peer), device_id_type=MESH,
            ).start()
        breathe()
        drain(reduce_in.at[step, 0 : NCOL - 1], reduce_sem.at[step, 1])
        mine = jnp.sum(reduce_in[step].astype(F32), axis=0)
        gather_in[step, pl.ds(me, 1)] = mine.astype(BF16)[None]
        for peer in peers:
            pltpu.make_async_remote_copy(
                src_ref=gather_in.at[step, me], dst_ref=gather_in.at[step, me],
                send_sem=gather_sem.at[step, 0], recv_sem=gather_sem.at[step, 1], device_id=(row, peer), device_id_type=MESH,
            ).start()
        breathe()
        drain(reduce_in.at[step, 0 : NCOL - 1], reduce_sem.at[step, 0])
        drain(gather_in.at[step, 0 : NCOL - 1], gather_sem.at[step, 1])

    def begin_gram(step):
        packed = gather_in[step].reshape(NCOL * half, 128)
        sample_t[...] = packed.astype(F32).T.astype(BF16)
        gram = dot(sample_t[...], packed)
        gram = gram[0:RANK] + pltpu.roll(gram[RANK : 2 * RANK], RANK, 1)
        gram_out[step] = gram
        gram_in[step, pl.ds(row, 1)] = gram[None]
        for other in (1, 2, 3):
            pltpu.make_async_remote_copy(
                src_ref=gram_out.at[step], dst_ref=gram_in.at[step, row],
                send_sem=gram_sem.at[step, 0], recv_sem=gram_sem.at[step, 1],
                device_id=((row + other) % 4, me), device_id_type=MESH,
            ).start()

    def end_gram(step):
        drain(gram_in.at[step, 0:3], gram_sem.at[step, 1])
        drain(gram_in.at[step, 0:3], gram_sem.at[step, 0])
        gram = (gram_in[step, 0] + gram_in[step, 1]) + (gram_in[step, 2] + gram_in[step, 3])
        lanes = lax.broadcasted_iota(jnp.int32, (RANK, 128), 1)
        subs = lax.broadcasted_iota(jnp.int32, (RANK, 128), 0)
        work[...] = jnp.where(lanes < RANK, gram, jnp.where(lanes - RANK == subs, 1.0, 0.0))

    def eliminate(first, last):
        lanes = lax.broadcasted_iota(jnp.int32, (RANK, 128), 1)
        subs = lax.broadcasted_iota(jnp.int32, (RANK, 1), 0)

        def pivot(k, carry):
            held = work[...]
            line = work[pl.ds(k, 1), :]
            column = jnp.sum(jnp.where(lanes == k, held, 0.0), axis=1, keepdims=True)
            top = jnp.sum(jnp.where(lanes[0:1] == k, line, 0.0), axis=1, keepdims=True)
            scaled = jnp.where(subs > k, column, 0.0) * (1.0 / top)
            work[...] = held - scaled * line
            return carry

        lax.fori_loop(first, last, pivot, 0)

    def inverse_factor():
        lanes = lax.broadcasted_iota(jnp.int32, (RANK, 128), 1)
        subs = lax.broadcasted_iota(jnp.int32, (RANK, 128), 0)
        held = work[...]
        pivots = jnp.sum(jnp.where(lanes == subs, held, 0.0), axis=1, keepdims=True)
        return jnp.where(lanes < RANK, 0.0, held * (1.0 / jnp.sqrt(pivots)))

    def project_all(step):
        project[...] = jnp.zeros(project.shape, F32)

        def some(part, carry):
            blocks = pl.ds(pl.multiple_of(part * 16, 16), 16)
            depth = pl.ds(pl.multiple_of(part * 16 * half, 128), 16 * half)
            top = res[blocks, 0].reshape(16 * half, cols)
            bottom = res[blocks, 1].reshape(16 * half, cols)
            project[...] += dot(sample_t[0:RANK, depth], top) + dot(sample_t[RANK : 2 * RANK, depth], bottom)
            return carry

        lax.fori_loop(0, NCOL // 16, some, 0)

    def reduce_project(step):
        part = RANK // 2
        mine = pl.ds(pl.multiple_of(core * part, part), part)
        other = pl.ds(pl.multiple_of((1 - core) * part, part), part)
        one = pltpu.make_async_remote_copy(
            src_ref=project.at[other, :], dst_ref=half_in.at[step],
            send_sem=half_sem.at[step, 0], recv_sem=half_sem.at[step, 1], device_id=(mate, me), device_id_type=MESH,
        )
        one.start()
        breathe()
        end_gram(step)
        one.wait()
        project[mine, :] = project[mine, :] + half_in[step]
        two = pltpu.make_async_remote_copy(
            src_ref=project.at[mine, :], dst_ref=pair_in.at[step],
            send_sem=pair_sem.at[step, 0], recv_sem=pair_sem.at[step, 1], device_id=(across, me), device_id_type=MESH,
        )
        two.start()
        breathe()
        eliminate(0, RANK // 2)
        two.wait()
        total[step, mine, :] = project[mine, :] + pair_in[step]
        three = pltpu.make_async_remote_copy(
            src_ref=total.at[step, mine, :], dst_ref=total.at[step, mine, :],
            send_sem=total_sem.at[step, 0], recv_sem=total_sem.at[step, 1], device_id=(mate, me), device_id_type=MESH,
        )
        three.start()
        breathe()
        eliminate(RANK // 2, RANK)
        three.wait()

    root = math.sqrt(ROWS)
    for step in range(POWER + 1):
        sample(step)
        if step == 0:
            for copy in own:
                copy.start()
        begin_gram(step)
        project_all(step)
        reduce_project(step)
        inverse = inverse_factor()
        factor = dot(pltpu.roll(inverse, RANK, 1)[:, 0:RANK], total[step], HIGH)
        if step < POWER:
            upper = factor.astype(BF16)
            lower = (factor - upper.astype(F32)).astype(BF16)
            factor_top[0:RANK, :] = upper
            factor_top[2 * RANK : 3 * RANK, :] = lower
            factor_bot[RANK : 2 * RANK, :] = upper
            factor_bot[3 * RANK : 4 * RANK, :] = lower
        else:
            lora_b[...] = factor * (1.0 / root)
            packed = gather_in[step].reshape(NCOL * half, 128).astype(F32)
            right = inverse * root
            left = pltpu.roll(right, RANK, 1)
            lora_a[:, 0] = dot_nt(packed, left, HIGH).reshape(NCOL, half, RANK)
            lora_a[:, 1] = dot_nt(packed, right, HIGH).reshape(NCOL, half, RANK)
        drain(gather_in.at[step, 0 : NCOL - 1], gather_sem.at[step, 0])
    breathe(last=True)

    for copy in own:
        copy.wait()
    drain(scale_out.at[0 : NCOL - 1], scale_sem.at[0])
    drain(scales.at[0 : NCOL - 1], scale_sem.at[1])
    drain(deq.at[0 : NCOL - 1], block_sem.at[0])
    drain(quant.at[:, pl.ds(0, (NCOL - 1) * cols)], block_sem.at[1])


def body(weight, sketch, codebook):
    rows, cols = weight.shape
    per_block = rows // NCOL
    half = per_block // 2
    steps = POWER + 1
    anywhere = pl.BlockSpec(memory_space=pl.ANY)
    local = pl.BlockSpec(memory_space=pltpu.VMEM)
    dma = pltpu.SemaphoreType.DMA
    quant, scales, lora_a, lora_b = pl.pallas_call(
        kernel,
        name="loftq",
        out_shape=(
            jax.ShapeDtypeStruct((per_block, NCOL * cols), BF16),
            jax.ShapeDtypeStruct((NCOL, 32, 128), BF16),
            jax.ShapeDtypeStruct((NCOL, 2, half, RANK), F32),
            jax.ShapeDtypeStruct((RANK, cols), F32),
        ),
        in_specs=[anywhere, local, pl.BlockSpec(memory_space=pltpu.SMEM)],
        out_specs=(anywhere, anywhere, local, local),
        scratch_shapes=[
            pltpu.VMEM((NCOL, per_block, cols), BF16),
            pltpu.VMEM((NCOL, 2, half, cols), BF16),
            pltpu.VMEM((NCOL, 32, 128), BF16),
            pltpu.VMEM((4 * RANK, cols), BF16),
            pltpu.VMEM((4 * RANK, cols), BF16),
            pltpu.VMEM((NCOL, half, 128), BF16),
            pltpu.VMEM((steps, NCOL, half, 128), BF16),
            pltpu.VMEM((steps, NCOL, half, 128), BF16),
            pltpu.VMEM((128, NCOL * half), BF16),
            pltpu.VMEM((RANK, cols), F32),
            pltpu.VMEM((steps, RANK // 2, cols), F32),
            pltpu.VMEM((steps, RANK // 2, cols), F32),
            pltpu.VMEM((steps, RANK, cols), F32),
            pltpu.VMEM((steps, 4, RANK, 128), F32),
            pltpu.VMEM((steps, RANK, 128), F32),
            pltpu.VMEM((RANK, 128), F32),
            dma((NCOL,)),
            dma((2,)),
            dma((2,)),
            dma((2,)),
            dma((steps, 2)),
            dma((steps, 2)),
            dma((steps, 2)),
            dma((steps, 2)),
            dma((steps, 2)),
            dma((steps, 2)),
        ],
        compiler_params=pltpu.CompilerParams(
            collective_id=0, has_side_effects=True, vmem_limit_bytes=56 * 1024 * 1024
        ),
    )(weight, sketch, codebook.astype(F32))
    blocks = cols // BLOCK
    scales = scales[:, :, :96].reshape(NCOL, 32, 3, 32)[..., :blocks]
    scales = scales.transpose(2, 1, 0, 3).reshape(per_block, NCOL * blocks).astype(F32)
    return quant, scales, lora_a.reshape(rows, RANK), lora_b


def solution(mesh):
    in_specs = (P("row", "col"), P("col", None), P())
    out_specs = (P(("row", "col"), None), P(("row", "col"), None), P("row", None), P(None, "col"))
    return jax.shard_map(body, mesh=mesh, in_specs=in_specs, out_specs=out_specs, check_vma=False)
```

time: 1480 us -> 273 us (0.18)
  waiting for transfers between devices: 1030 us -> 0 us
  Pallas kernels: 0 us -> 251 us
  matrix products: 133 us -> 0 us
  other arithmetic: 118 us -> 1.39 us
  blocking collectives: 108 us -> 0 us
  local copies, waits for them, and re-layouts: 41.9 us -> 19.1 us
  starting transfers between devices: 16.9 us -> 0 us
    psum x6 -> x0, waiting for transfers between devices: 1030 us -> none  [the longest x3 843 us: orthonormal(): sample = lax.psum(partial_sample, 'col')]
    pallas_call x0 -> x1, Pallas kernels: none -> 251 us  [body(): pl.pallas_call(kernel, name='loftq', out_shape=(jax.ShapeDtypeStruct((per...]
    dot_general x9 -> x0, matrix products: 127 us -> none  [the longest x3 70.8 us: projection(): jnp.dot(residual.T, basis, precision=high, preferred_element_type=jnp.flo...]
    psum x3 -> x0, blocking collectives: 108 us -> none  [orthonormal(): lax.psum(jnp.dot(sample.T, sample, precision=high, preferred_element_type...]
    sub x1 -> x0, other arithmetic: 56 us -> none  [body(): residual = weight.astype(jnp.float32) - dequant]
    another operation x15 -> x0, other arithmetic: 36.2 us -> none  [the longest x9 19.6 us: solve_basis(): lower = jnp.linalg.cholesky(gram)]
    all_to_all x2 -> x0, starting transfers between devices: 16.2 us -> none  [the longest x1 9.22 us: body(): lax.all_to_all(tile_scales.astype(jnp.bfloat16), 'col', split_axis=0, con...]
  transfers between devices with their start and end apart: 8 -> 0, of which waited for: 6 -> 0; matrix products, arithmetic and copies ran while one was open for 12% -> 0% of each run, Pallas kernels for 0% -> 0%
where the time goes in v1:
time: 273 us; the launch traced here: 272 us
  Pallas kernels  251 us (92%)
  local copies, waits for them, and re-layouts  19.1 us (7%)
    pallas_call x1, Pallas kernels, body(): pl.pallas_call(kernel, name='loftq', out_shape=(jax.ShapeDtypeStruct((per...  251 us
    unnamed x6, local copies, waits for them, and re-layouts  14 us

profile of v1, /device:TPU:1, one launch (start us, length us, event | category | flops | bytes accessed | tf_op | source)
XLA Modules:
  0.0 272.3 jit_solution(9739865065348411659)
XLA Ops:
  0.6 1.2 convert_element_type.12.codebook
  1.8 1.9 copy.10.sketch
  3.7 251.2 %loftq.1 = (bf16[96,53248]{1,0:T(8,128)(2,1)}, bf16[32,32,128]{2,1,0:T(8,128)(2,1)}, f32[32,2,48,64]{3,2,1,0:T(8,128)}, f32[64,1664]{1,0:T(8,128)}) custom-call(bf16[3072,1664]{1,0:T(8,128)(2,1)} %weight.1, bf16[1664,64]{1,0:T(8,128)(2,1)} %copy.10.sketch, f32[16]{0:T(128)} %convert_element_type.12.codebook), custom_call_target="tpu_custom_call" | custom-call | tf_op jit(solution)/shard_map/loftq/pallas_call | solution.py:348
  254.9 2.4 reshape.17
  257.3 2.7 %copy.12 = f32[3072,64]{0,1:T(8,128)} copy(f32[3072,64]{1,0:T(8,128)} %bitcast.6) | data formatting | bytes 1572864
  260.0 0.2 convert_bitcast_fusion
  260.3 0.9 copy.11
  261.2 1.8 reshape.19
  263.0 0.0 copy-start
  263.0 8.6 %copy.15 = bf16[96,53248]{1,0:T(8,128)(2,1)} copy(bf16[96,53248]{1,0:T(8,128)(2,1)} %get-tuple-element.24) | data formatting | bytes 20447232
  271.6 0.0 copy-done
  271.6 0.8 copy.16
Async XLA Ops:
  263.0 8.6 %copy-start = (f32[64,1664]{1,0:T(8,128)S(1)}, f32[64,1664]{1,0:T(8,128)}, u32[]{:S(2)}) copy-start(f32[64,1664]{1,0:T(8,128)} %get-tuple-element.27) | copy-start | bytes 1277956

commit v2 on v1

--- a/solution.py
+++ b/solution.py
@@ -21,25 +21,28 @@
 
 ROUNDS = (
     ((1, 1, 0), (3, 3, 1)),
+    ((1, 1, 1), (3, 3, 0)),
+    ((1, 3, 0), (3, 1, 1)),
+    ((1, 3, 1), (3, 1, 0)),
     ((2, 0, 0), (0, 2, 1)),
-    ((1, 3, 0), (3, 1, 1)),
+    ((2, 0, 1), (0, 2, 0)),
     ((2, 1, 0), (0, 3, 1)),
+    ((2, 1, 1), (0, 3, 0)),
+    ((2, 3, 0), (0, 1, 1)),
+    ((2, 3, 1), (0, 1, 0)),
     ((1, 2, 0), (3, 0, 1)),
+    ((1, 2, 1), (3, 0, 0)),
+    ((3, 2, 0), (1, 0, 1)),
+    ((3, 2, 1), (1, 0, 0)),
     ((2, 2, 1),),
-    ((1, 1, 1), (3, 3, 0)),
-    ((2, 3, 0), (0, 1, 1)),
-    ((3, 2, 0), (1, 0, 1)),
-    ((2, 0, 1), (0, 2, 0)),
-    ((1, 3, 1), (3, 1, 0)),
-    ((2, 1, 1), (0, 3, 0)),
-    ((1, 2, 1), (3, 0, 0)),
-    ((2, 3, 1), (0, 1, 0)),
-    ((3, 2, 1), (1, 0, 0)),
     ((2, 2, 0), (0, 0, 1)),
 )
 CODES = tuple(dx + 4 * dy + 16 * dz for group in ROUNDS for dx, dy, dz in group)
-EARLY = 8
-PACE = (2, 2, 2, 1, 1, 2, 2, 2, 1, 1, 2, 2, 1, 1, 1)
+EARLY = 6
+SPACING = 5
+CUTS = 3
+PACE = (0, 0, 0, 1, 0, 0, 2) + (1, 0, 0, 1, 0, 0, 2) * 2
+WINDOW = 6
 
 
 def partner(me, code):
@@ -71,8 +74,8 @@
     weight, sketch, codebook,
     quant, scales, lora_a, lora_b,
     deq, res, scale_out, factor_top, factor_bot, sample_out, reduce_in, gather_in, sample_t,
-    project, half_in, pair_in, total, gram_in, gram_out, work,
-    load_sem, block_sem, scale_sem, own_sem, reduce_sem, gather_sem, half_sem, pair_sem, total_sem, gram_sem,
+    project, half_in, pair_out, pair_in, last_out, last_in, total, gram_in, gram_out, work,
+    load_sem, block_sem, scale_sem, own_sem, reduce_sem, gather_sem, half_sem, pair_sem, total_sem, gram_sem, tail_sem,
 ):
     cols = deq.shape[2]
     tiles = cols // 128
@@ -101,10 +104,9 @@
     for other in (1, 2, 3):
         pl.semaphore_signal(barrier, inc=1, device_id=((row + other) % 4, me), device_id_type=MESH)
 
-    unit = (lax.broadcasted_iota(jnp.int32, (RANK, RANK), 0) == lax.broadcasted_iota(jnp.int32, (RANK, RANK), 1))
     factor_top[...] = jnp.zeros(factor_top.shape, BF16)
     factor_bot[...] = jnp.zeros(factor_bot.shape, BF16)
-    turned = dot_nt(unit.astype(BF16), sketch[...]).astype(BF16)
+    turned = sketch[...]
     factor_top[0:RANK, :] = turned
     factor_bot[RANK : 2 * RANK, :] = turned
 
@@ -116,12 +118,17 @@
 
     pl.semaphore_wait(barrier, len(peers) + 3)
 
-    def send_block(place, peer):
-        blocks = pltpu.make_async_remote_copy(
-            src_ref=deq.at[peer], dst_ref=quant.at[:, pl.ds(pl.multiple_of(me * cols, 128), cols)],
-            send_sem=block_sem.at[0], recv_sem=block_sem.at[1], device_id=(row, peer), device_id_type=MESH,
+    def send_rows(peer, first, count, sem=None):
+        rows = slice(first, first + count)
+        copy = pltpu.make_async_remote_copy(
+            src_ref=deq.at[peer, rows], dst_ref=quant.at[rows, pl.ds(pl.multiple_of(me * cols, 128), cols)],
+            send_sem=block_sem.at[0] if sem is None else sem, recv_sem=block_sem.at[1],
+            device_id=(row, peer), device_id_type=MESH,
         )
-        blocks.start()
+        copy.start()
+        return copy
+
+    def send_scales(peer):
         pltpu.make_async_remote_copy(
             src_ref=scale_out.at[peer], dst_ref=scales.at[me],
             send_sem=scale_sem.at[0], recv_sem=scale_sem.at[1], device_id=(row, peer), device_id_type=MESH,
@@ -160,9 +167,12 @@
 
         lax.fori_loop(0, per_block // 16, quantize_rows, 0)
 
-        @pl.when(place < EARLY)
+        @pl.when((place % SPACING == 1) & (place // SPACING < EARLY))
         def _():
-            send_block(place, block)
+            for member in range(2):
+                peer = partner(me, code_at(place // SPACING * 2 + member))
+                send_rows(peer, 0, per_block)
+                send_scales(peer)
 
         return carry
 
@@ -174,32 +184,62 @@
         pltpu.make_async_copy(scale_out.at[me], scales.at[me], own_sem.at[1]),
     ]
 
-    state = {"sent": EARLY, "point": 0}
-
-    def breathe(last=False):
-        count = len(CODES) if last else PACE[state["point"]]
+    rounds, place = [], 0
+    for group in ROUNDS:
+        rounds.append(peers[place : place + len(group)])
+        place += len(group)
+    rounds = rounds[EARLY:]
+    pieces = [(group, cut) for group in rounds for cut in range(CUTS)]
+    state = {"sent": 0, "point": 0}
+
+    def breathe():
+        count = PACE[state["point"]]
         state["point"] += 1
-        for place in range(state["sent"], min(state["sent"] + count, len(CODES))):
-            send_block(place, peers[place])
-            state["sent"] = place + 1
+        for group, cut in pieces[state["sent"] : state["sent"] + count]:
+            for peer in group:
+                send_rows(peer, cut * (per_block // CUTS), per_block // CUTS)
+                if cut == 0:
+                    send_scales(peer)
+        state["sent"] += count
+
+    def send_rest():
+        rest = [(peer, cut) for group, cut in pieces[state["sent"] :] for peer in group]
+        copies = []
+        for place, (peer, cut) in enumerate(rest):
+            if place >= WINDOW:
+                copies[place - WINDOW].wait_send()
+            copies.append(send_rows(peer, cut * (per_block // CUTS), per_block // CUTS, tail_sem.at[place % WINDOW]))
+            if cut == 0:
+                send_scales(peer)
+        for copy in copies[-WINDOW:]:
+            copy.wait_send()
+        return len(rest) * (per_block // CUTS)
 
     def sample(step):
-        def some(part, carry):
+        breathe()
+        def some(turn, carry):
+            part = (me // 8 + turn + 1) % 4
             blocks = pl.ds(pl.multiple_of(part * 8, 8), 8)
             top = res[blocks, 0].reshape(8 * half, cols)
             bottom = res[blocks, 1].reshape(8 * half, cols)
             both = dot_nt(top, factor_top[...]) + dot_nt(bottom, factor_bot[...])
             both = both[:, 0:128] + both[:, 128:256]
             sample_out[blocks] = both.reshape(8, half, 128).astype(BF16)
+            for near in range(7, -1, -1):
+                peer = part * 8 + (me // 4 + near // 4) % 2 * 4 + (me + near) % 4
+
+                @pl.when(peer != me)
+                def _():
+                    pltpu.make_async_remote_copy(
+                        src_ref=sample_out.at[peer], dst_ref=reduce_in.at[step, me],
+                        send_sem=reduce_sem.at[step, 0], recv_sem=reduce_sem.at[step, 1],
+                        device_id=(row, peer), device_id_type=MESH,
+                    ).start()
+
             return carry
 
         lax.fori_loop(0, NCOL // 8, some, 0)
         reduce_in[step, pl.ds(me, 1)] = sample_out[pl.ds(me, 1)]
-        for peer in peers:
-            pltpu.make_async_remote_copy(
-                src_ref=sample_out.at[peer], dst_ref=reduce_in.at[step, me],
-                send_sem=reduce_sem.at[step, 0], recv_sem=reduce_sem.at[step, 1], device_id=(row, peer), device_id_type=MESH,
-            ).start()
         breathe()
         drain(reduce_in.at[step, 0 : NCOL - 1], reduce_sem.at[step, 1])
         mine = jnp.sum(reduce_in[step].astype(F32), axis=0)
@@ -258,6 +298,7 @@
         return jnp.where(lanes < RANK, 0.0, held * (1.0 / jnp.sqrt(pivots)))
 
     def project_all(step):
+        breathe()
         project[...] = jnp.zeros(project.shape, F32)
 
         def some(part, carry):
@@ -282,16 +323,17 @@
         breathe()
         end_gram(step)
         one.wait()
-        project[mine, :] = project[mine, :] + half_in[step]
+        sent, met = (pair_out, pair_in.at[step]) if step < POWER else (last_out, last_in)
+        sent[...] = (project[mine, :] + half_in[step]).astype(sent.dtype)
         two = pltpu.make_async_remote_copy(
-            src_ref=project.at[mine, :], dst_ref=pair_in.at[step],
+            src_ref=sent, dst_ref=met,
             send_sem=pair_sem.at[step, 0], recv_sem=pair_sem.at[step, 1], device_id=(across, me), device_id_type=MESH,
         )
         two.start()
         breathe()
         eliminate(0, RANK // 2)
         two.wait()
-        total[step, mine, :] = project[mine, :] + pair_in[step]
+        total[step, mine, :] = sent[...].astype(F32) + met[...].astype(F32)
         three = pltpu.make_async_remote_copy(
             src_ref=total.at[step, mine, :], dst_ref=total.at[step, mine, :],
             send_sem=total_sem.at[step, 0], recv_sem=total_sem.at[step, 1], device_id=(mate, me), device_id_type=MESH,
@@ -327,14 +369,48 @@
             lora_a[:, 0] = dot_nt(packed, left, HIGH).reshape(NCOL, half, RANK)
             lora_a[:, 1] = dot_nt(packed, right, HIGH).reshape(NCOL, half, RANK)
         drain(gather_in.at[step, 0 : NCOL - 1], gather_sem.at[step, 0])
-    breathe(last=True)
+    apart = send_rest()
 
     for copy in own:
         copy.wait()
     drain(scale_out.at[0 : NCOL - 1], scale_sem.at[0])
     drain(scales.at[0 : NCOL - 1], scale_sem.at[1])
-    drain(deq.at[0 : NCOL - 1], block_sem.at[0])
+    whole, over = divmod((NCOL - 1) * per_block - apart, per_block)
+    drain(deq.at[0:whole], block_sem.at[0])
+    if over:
+        drain(deq.at[0, 0:over], block_sem.at[0])
     drain(quant.at[:, pl.ds(0, (NCOL - 1) * cols)], block_sem.at[1])
+
+
+def finish(quant_in, pieces, basis, lora_b_in, quant, scales, lora_a, lora_b, held, sems):
+    strips = [slice(16 * k, 16 * k + 16) for k in range(quant.shape[0] // 16)]
+    loads = [pltpu.make_async_copy(quant_in.at[strip], held.at[strip], sems.at[0, k]) for k, strip in enumerate(strips)]
+    stores = [pltpu.make_async_copy(held.at[strip], quant.at[strip], sems.at[1, k]) for k, strip in enumerate(strips)]
+    for copy in loads:
+        copy.start()
+    lora_b[...] = lora_b_in[...]
+    lora_a[...] = basis[...].T
+    width = scales.shape[1] // NCOL
+    lane = lax.broadcasted_iota(jnp.int32, (32, 128), 1)
+    for group in range(scales.shape[0] // 32):
+        for load, store in zip(loads[2 * group : 2 * group + 2], stores[2 * group : 2 * group + 2]):
+            load.wait()
+            store.start()
+        rows = slice(32 * group, 32 * group + 32)
+        found = [jnp.zeros((32, 128), F32) for _ in range(scales.shape[1] // 128 + 1)]
+        for source in range(NCOL):
+            start = source * width
+            tile, first = start // 128, start % 128
+            turned = pltpu.roll(pieces[source].astype(F32), (first - 32 * group) % 128, 1)
+            found[tile] = jnp.where((lane >= first) & (lane < first + width), turned, found[tile])
+            if first + width > 128:
+                found[tile + 1] = jnp.where(lane < first + width - 128, turned, found[tile + 1])
+        for tile, part in enumerate(found):
+            left = min(128, scales.shape[1] - 128 * tile)
+            if left > 0:
+                scales[rows, 128 * tile : 128 * tile + left] = part[:, :left]
+    for copy in stores:
+        copy.wait()
 
 
 def body(weight, sketch, codebook):
@@ -368,7 +444,10 @@
             pltpu.VMEM((128, NCOL * half), BF16),
             pltpu.VMEM((RANK, cols), F32),
             pltpu.VMEM((steps, RANK // 2, cols), F32),
-            pltpu.VMEM((steps, RANK // 2, cols), F32),
+            pltpu.VMEM((RANK // 2, cols), BF16),
+            pltpu.VMEM((POWER, RANK // 2, cols), BF16),
+            pltpu.VMEM((RANK // 2, cols), F32),
+            pltpu.VMEM((RANK // 2, cols), F32),
             pltpu.VMEM((steps, RANK, cols), F32),
             pltpu.VMEM((steps, 4, RANK, 128), F32),
             pltpu.VMEM((steps, RANK, 128), F32),
@@ -383,15 +462,27 @@
             dma((steps, 2)),
             dma((steps, 2)),
             dma((steps, 2)),
+            dma((WINDOW,)),
         ],
         compiler_params=pltpu.CompilerParams(
             collective_id=0, has_side_effects=True, vmem_limit_bytes=56 * 1024 * 1024
         ),
-    )(weight, sketch, codebook.astype(F32))
-    blocks = cols // BLOCK
-    scales = scales[:, :, :96].reshape(NCOL, 32, 3, 32)[..., :blocks]
-    scales = scales.transpose(2, 1, 0, 3).reshape(per_block, NCOL * blocks).astype(F32)
-    return quant, scales, lora_a.reshape(rows, RANK), lora_b
+    )(weight, sketch.T, codebook.astype(F32))
+    quant, scales, lora_a, lora_b = pl.pallas_call(
+        finish,
+        name="finish",
+        out_shape=(
+            jax.ShapeDtypeStruct((per_block, NCOL * cols), BF16),
+            jax.ShapeDtypeStruct((per_block, NCOL * cols // BLOCK), F32),
+            jax.ShapeDtypeStruct((RANK, rows), F32),
+            jax.ShapeDtypeStruct((RANK, cols), F32),
+        ),
+        in_specs=[anywhere, local, local, local],
+        out_specs=(anywhere, local, local, local),
+        scratch_shapes=[pltpu.VMEM((per_block, NCOL * cols), BF16), dma((2, per_block // 16))],
+        compiler_params=pltpu.CompilerParams(vmem_limit_bytes=58 * 1024 * 1024),
+    )(quant, scales, lora_a.reshape(rows, RANK), lora_b)
+    return quant, scales, lora_a.T, lora_b
 
 
 def solution(mesh):

time: 273 us -> 232 us (0.85)
  Pallas kernels: 251 us -> 230 us
  local copies, waits for them, and re-layouts: 19.1 us -> 0 us
    pallas_call x1, Pallas kernels: 251 us -> 220 us  [body(): pl.pallas_call(kernel, name='loftq', out_shape=(jax.ShapeDtypeStruct((per...]
    unnamed x6 -> x0, local copies, waits for them, and re-layouts: 14 us -> none
    pallas_call x0 -> x1, Pallas kernels: none -> 10.7 us  [body(): pl.pallas_call(finish, name='finish', out_shape=(jax.ShapeDtypeStruct((pe...]
where the time goes in v2:
time: 232 us
  Pallas kernels  230 us (99%)
    pallas_call x1, Pallas kernels, body(): pl.pallas_call(kernel, name='loftq', out_shape=(jax.ShapeDtypeStruct((per...  220 us
    pallas_call x1, Pallas kernels, body(): pl.pallas_call(finish, name='finish', out_shape=(jax.ShapeDtypeStruct((pe...  10.7 us

profile of v2, /device:TPU:1, one launch (start us, length us, event | category | flops | bytes accessed | tf_op | source)
XLA Modules:
  0.0 232.1 jit_solution(4962228871642968807)
XLA Ops:
  0.6 1.2 convert_element_type.3.codebook
  1.8 219.6 %loftq.1 = (bf16[96,53248]{1,0:T(8,128)(2,1)}, bf16[32,32,128]{2,1,0:T(8,128)(2,1)}, f32[32,2,48,64]{3,2,1,0:T(8,128)}, f32[64,1664]{1,0:T(8,128)}) custom-call(bf16[3072,1664]{1,0:T(8,128)(2,1)} %weight.1, bf16[64,1664]{1,0:T(8,128)(2,1)} %bitcast.4, f32[16]{0:T(128)} %convert_element_type.3.codebook), custom_call_target="tpu_custom_call" | custom-call | tf_op jit(solution)/shard_map/loftq/pallas_call | solution.py:424
  221.4 10.7 %finish.1 = (bf16[96,53248]{1,0:T(8,128)(2,1)}, f32[96,832]{1,0:T(8,128)}, f32[64,3072]{1,0:T(8,128)}, f32[64,1664]{1,0:T(8,128)}) custom-call(bf16[96,53248]{1,0:T(8,128)(2,1)} %get-tuple-element.12.quant_in, bf16[32,32,128]{2,1,0:T(8,128)(2,1)} %get-tuple-element.13.pieces, f32[3072,64]{1,0:T(8,128)} %bitcast.3, f32[64,1664]{1,0:T(8,128)} %get-tuple-element.15.lora_b_in), custom_call_target="tpu_custom_call" | custom-call | tf_op jit(solution)/shard_map/finish/pallas_call | solution.py:471

commit v3 on v2

--- a/solution.py
+++ b/solution.py
@@ -40,9 +40,9 @@
 CODES = tuple(dx + 4 * dy + 16 * dz for group in ROUNDS for dx, dy, dz in group)
 EARLY = 6
 SPACING = 5
-CUTS = 3
-PACE = (0, 0, 0, 1, 0, 0, 2) + (1, 0, 0, 1, 0, 0, 2) * 2
-WINDOW = 6
+CUTS = 6
+PACE = (0, 0, 1, 2, 0, 2, 4) * 3
+WINDOW = 12
 
 
 def partner(me, code):
@@ -73,7 +73,7 @@
 def kernel(
     weight, sketch, codebook,
     quant, scales, lora_a, lora_b,
-    deq, res, scale_out, factor_top, factor_bot, sample_out, reduce_in, gather_in, sample_t,
+    deq, res, scale_out, scale_in, basis, factor_top, factor_bot, sample_out, reduce_in, gather_in, sample_t,
     project, half_in, pair_out, pair_in, last_out, last_in, total, gram_in, gram_out, work,
     load_sem, block_sem, scale_sem, own_sem, reduce_sem, gather_sem, half_sem, pair_sem, total_sem, gram_sem, tail_sem,
 ):
@@ -130,7 +130,7 @@
 
     def send_scales(peer):
         pltpu.make_async_remote_copy(
-            src_ref=scale_out.at[peer], dst_ref=scales.at[me],
+            src_ref=scale_out.at[peer], dst_ref=scale_in.at[me],
             send_sem=scale_sem.at[0], recv_sem=scale_sem.at[1], device_id=(row, peer), device_id_type=MESH,
         ).start()
 
@@ -181,7 +181,7 @@
 
     own = [
         pltpu.make_async_copy(deq.at[me], quant.at[:, pl.ds(pl.multiple_of(me * cols, 128), cols)], own_sem.at[0]),
-        pltpu.make_async_copy(scale_out.at[me], scales.at[me], own_sem.at[1]),
+        pltpu.make_async_copy(scale_out.at[me], scale_in.at[me], own_sem.at[1]),
     ]
 
     rounds, place = [], 0
@@ -202,18 +202,44 @@
                     send_scales(peer)
         state["sent"] += count
 
-    def send_rest():
-        rest = [(peer, cut) for group, cut in pieces[state["sent"] :] for peer in group]
-        copies = []
-        for place, (peer, cut) in enumerate(rest):
-            if place >= WINDOW:
-                copies[place - WINDOW].wait_send()
-            copies.append(send_rows(peer, cut * (per_block // CUTS), per_block // CUTS, tail_sem.at[place % WINDOW]))
+    rest = []
+
+    def begin_rest():
+        for group, cut in pieces[state["sent"] :]:
+            rest.extend((peer, cut) for peer in group)
+        for peer, cut in rest:
             if cut == 0:
                 send_scales(peer)
-        for copy in copies[-WINDOW:]:
-            copy.wait_send()
-        return len(rest) * (per_block // CUTS)
+        tail.extend(send_tail(place) for place in range(min(WINDOW, len(rest))))
+
+    tail = []
+
+    def send_tail(place):
+        peer, cut = rest[place]
+        return send_rows(peer, cut * (per_block // CUTS), per_block // CUTS, tail_sem.at[place % WINDOW])
+
+    def end_rest():
+        for place in range(WINDOW, len(rest)):
+            tail[place - WINDOW].wait_send()
+            tail.append(send_tail(place))
+
+    def place_scales():
+        width = scales.shape[1] // NCOL
+        lanes = lax.broadcasted_iota(jnp.int32, (32, 128), 1)
+        for group in range(per_block // 32):
+            rows = slice(32 * group, 32 * group + 32)
+            found = [jnp.zeros((32, 128), F32) for _ in range(scales.shape[1] // 128 + 1)]
+            for source in range(NCOL):
+                start = source * width
+                tile, first = start // 128, start % 128
+                turned = pltpu.roll(scale_in[source].astype(F32), (first - 32 * group) % 128, 1)
+                found[tile] = jnp.where((lanes >= first) & (lanes < first + width), turned, found[tile])
+                if first + width > 128:
+                    found[tile + 1] = jnp.where(lanes < first + width - 128, turned, found[tile + 1])
+            for tile, part in enumerate(found):
+                left = min(128, scales.shape[1] - 128 * tile)
+                if left > 0:
+                    scales[rows, 128 * tile : 128 * tile + left] = part[:, :left]
 
     def sample(step):
         breathe()
@@ -362,19 +388,24 @@
             factor_bot[RANK : 2 * RANK, :] = upper
             factor_bot[3 * RANK : 4 * RANK, :] = lower
         else:
+            begin_rest()
             lora_b[...] = factor * (1.0 / root)
             packed = gather_in[step].reshape(NCOL * half, 128).astype(F32)
             right = inverse * root
             left = pltpu.roll(right, RANK, 1)
-            lora_a[:, 0] = dot_nt(packed, left, HIGH).reshape(NCOL, half, RANK)
-            lora_a[:, 1] = dot_nt(packed, right, HIGH).reshape(NCOL, half, RANK)
+            basis[:, 0] = dot_nt(packed, left, HIGH).reshape(NCOL, half, RANK)
+            basis[:, 1] = dot_nt(packed, right, HIGH).reshape(NCOL, half, RANK)
+            lora_a[...] = basis[...].reshape(lora_a.shape[1], RANK).T
         drain(gather_in.at[step, 0 : NCOL - 1], gather_sem.at[step, 0])
-    apart = send_rest()
-
+    end_rest()
     for copy in own:
         copy.wait()
     drain(scale_out.at[0 : NCOL - 1], scale_sem.at[0])
-    drain(scales.at[0 : NCOL - 1], scale_sem.at[1])
+    drain(scale_in.at[0 : NCOL - 1], scale_sem.at[1])
+    place_scales()
+    for copy in tail[-WINDOW:]:
+        copy.wait_send()
+    apart = len(rest) * (per_block // CUTS)
     whole, over = divmod((NCOL - 1) * per_block - apart, per_block)
     drain(deq.at[0:whole], block_sem.at[0])
     if over:
@@ -382,35 +413,22 @@
     drain(quant.at[:, pl.ds(0, (NCOL - 1) * cols)], block_sem.at[1])
 
 
-def finish(quant_in, pieces, basis, lora_b_in, quant, scales, lora_a, lora_b, held, sems):
-    strips = [slice(16 * k, 16 * k + 16) for k in range(quant.shape[0] // 16)]
-    loads = [pltpu.make_async_copy(quant_in.at[strip], held.at[strip], sems.at[0, k]) for k, strip in enumerate(strips)]
-    stores = [pltpu.make_async_copy(held.at[strip], quant.at[strip], sems.at[1, k]) for k, strip in enumerate(strips)]
-    for copy in loads:
-        copy.start()
-    lora_b[...] = lora_b_in[...]
-    lora_a[...] = basis[...].T
-    width = scales.shape[1] // NCOL
-    lane = lax.broadcasted_iota(jnp.int32, (32, 128), 1)
-    for group in range(scales.shape[0] // 32):
-        for load, store in zip(loads[2 * group : 2 * group + 2], stores[2 * group : 2 * group + 2]):
-            load.wait()
-            store.start()
-        rows = slice(32 * group, 32 * group + 32)
-        found = [jnp.zeros((32, 128), F32) for _ in range(scales.shape[1] // 128 + 1)]
-        for source in range(NCOL):
-            start = source * width
-            tile, first = start // 128, start % 128
-            turned = pltpu.roll(pieces[source].astype(F32), (first - 32 * group) % 128, 1)
-            found[tile] = jnp.where((lane >= first) & (lane < first + width), turned, found[tile])
-            if first + width > 128:
-                found[tile + 1] = jnp.where(lane < first + width - 128, turned, found[tile + 1])
-        for tile, part in enumerate(found):
-            left = min(128, scales.shape[1] - 128 * tile)
-            if left > 0:
-                scales[rows, 128 * tile : 128 * tile + left] = part[:, :left]
-    for copy in stores:
-        copy.wait()
+def finish(*refs):
+    count = len(refs) // 3
+    sources, targets, held, (load_sem, store_sem) = refs[:count], refs[count : 2 * count], refs[2 * count : 3 * count], refs[3 * count :]
+    strips = [(0, slice(16 * k, 16 * k + 16)) for k in range(sources[0].shape[0] // 16)]
+    strips += [(k, slice(0, sources[k].shape[0])) for k in range(1, count)]
+    loads, stores = [], []
+    for place, (k, rows) in enumerate(strips):
+        loads.append(pltpu.make_async_copy(sources[k].at[rows], held[k].at[rows], load_sem.at[place]))
+        stores.append(pltpu.make_async_copy(held[k].at[rows], targets[k].at[rows], store_sem.at[place]))
+    for load in loads:
+        load.start()
+    for load, store in zip(loads, stores):
+        load.wait()
+        store.start()
+    for store in stores:
+        store.wait()
 
 
 def body(weight, sketch, codebook):
@@ -426,16 +444,18 @@
         name="loftq",
         out_shape=(
             jax.ShapeDtypeStruct((per_block, NCOL * cols), BF16),
-            jax.ShapeDtypeStruct((NCOL, 32, 128), BF16),
-            jax.ShapeDtypeStruct((NCOL, 2, half, RANK), F32),
+            jax.ShapeDtypeStruct((per_block, NCOL * cols // BLOCK), F32),
+            jax.ShapeDtypeStruct((RANK, rows), F32),
             jax.ShapeDtypeStruct((RANK, cols), F32),
         ),
         in_specs=[anywhere, local, pl.BlockSpec(memory_space=pltpu.SMEM)],
-        out_specs=(anywhere, anywhere, local, local),
+        out_specs=(anywhere, local, local, local),
         scratch_shapes=[
             pltpu.VMEM((NCOL, per_block, cols), BF16),
             pltpu.VMEM((NCOL, 2, half, cols), BF16),
             pltpu.VMEM((NCOL, 32, 128), BF16),
+            pltpu.VMEM((NCOL, 32, 128), BF16),
+            pltpu.VMEM((NCOL, 2, half, RANK), F32),
             pltpu.VMEM((4 * RANK, cols), BF16),
             pltpu.VMEM((4 * RANK, cols), BF16),
             pltpu.VMEM((NCOL, half, 128), BF16),
@@ -468,20 +488,17 @@
             collective_id=0, has_side_effects=True, vmem_limit_bytes=56 * 1024 * 1024
         ),
     )(weight, sketch.T, codebook.astype(F32))
+    results = [quant, scales, lora_a, lora_b]
     quant, scales, lora_a, lora_b = pl.pallas_call(
         finish,
         name="finish",
-        out_shape=(
-            jax.ShapeDtypeStruct((per_block, NCOL * cols), BF16),
-            jax.ShapeDtypeStruct((per_block, NCOL * cols // BLOCK), F32),
-            jax.ShapeDtypeStruct((RANK, rows), F32),
-            jax.ShapeDtypeStruct((RANK, cols), F32),
-        ),
-        in_specs=[anywhere, local, local, local],
-        out_specs=(anywhere, local, local, local),
-        scratch_shapes=[pltpu.VMEM((per_block, NCOL * cols), BF16), dma((2, per_block // 16))],
+        out_shape=tuple(jax.ShapeDtypeStruct(result.shape, result.dtype) for result in results),
+        in_specs=[anywhere] * 4,
+        out_specs=(anywhere,) * 4,
+        scratch_shapes=[pltpu.VMEM(result.shape, result.dtype) for result in results]
+        + [dma((per_block // 16 + 3,)), dma((per_block // 16 + 3,))],
         compiler_params=pltpu.CompilerParams(vmem_limit_bytes=58 * 1024 * 1024),
-    )(quant, scales, lora_a.reshape(rows, RANK), lora_b)
+    )(*results)
     return quant, scales, lora_a.T, lora_b
 
 

time: 232 us -> 220 us (0.948)
  Pallas kernels: 230 us -> 218 us
    pallas_call x1, Pallas kernels: 220 us -> 209 us  [body(): pl.pallas_call(kernel, name='loftq', out_shape=(jax.ShapeDtypeStruct((per...]
where the time goes in v3:
time: 220 us
  Pallas kernels  218 us (99%)
    pallas_call x1, Pallas kernels, body(): pl.pallas_call(kernel, name='loftq', out_shape=(jax.ShapeDtypeStruct((per...  209 us
    pallas_call x1, Pallas kernels, body(): pl.pallas_call(finish, name='finish', out_shape=tuple((jax.ShapeDtypeStru...  8.53 us

profile of v3, /device:TPU:1, one launch (start us, length us, event | category | flops | bytes accessed | tf_op | source)
XLA Modules:
  0.0 219.7 jit_solution(3293978765372350930)
XLA Ops:
  0.6 1.2 convert_element_type.3.codebook
  1.8 209.4 %loftq.1 = (bf16[96,53248]{1,0:T(8,128)(2,1)}, f32[96,832]{1,0:T(8,128)}, f32[64,3072]{1,0:T(8,128)}, f32[64,1664]{1,0:T(8,128)}) custom-call(bf16[3072,1664]{1,0:T(8,128)(2,1)} %weight.1, bf16[64,1664]{1,0:T(8,128)(2,1)} %bitcast.2, f32[16]{0:T(128)} %convert_element_type.3.codebook), custom_call_target="tpu_custom_call" | custom-call | tf_op jit(solution)/shard_map/loftq/pallas_call | solution.py:442
  211.2 8.5 %finish.1 = (bf16[96,53248]{1,0:T(8,128)(2,1)}, f32[96,832]{1,0:T(8,128)}, f32[64,3072]{1,0:T(8,128)}, f32[64,1664]{1,0:T(8,128)}) custom-call(bf16[96,53248]{1,0:T(8,128)(2,1)} %get-tuple-element.12.refs_0_, f32[96,832]{1,0:T(8,128)} %get-tuple-element.13.refs_1_, f32[64,3072]{1,0:T(8,128)} %get-tuple-element.14.refs_2_, f32[64,1664]{1,0:T(8,128)} %get-tuple-element.15.refs_3_), custom_call_target="tpu_custom_call" | custom-call | tf_op jit(solution)/shard_map/finish/pallas_call | solution.py:492

commit v4 on v3

--- a/solution.py
+++ b/solution.py
@@ -38,8 +38,8 @@
     ((2, 2, 0), (0, 0, 1)),
 )
 CODES = tuple(dx + 4 * dy + 16 * dz for group in ROUNDS for dx, dy, dz in group)
-EARLY = 6
-SPACING = 5
+EARLY = 7
+SPACING = 4
 CUTS = 6
 PACE = (0, 0, 1, 2, 0, 2, 4) * 3
 WINDOW = 12

time: 220 us -> 224 us (1.018); the launches traced: 220 us -> 221 us
  no operation moved by 1% of the time
where the time goes in v4:
time: 224 us; the launch traced here: 221 us
  Pallas kernels  220 us (98%)
    pallas_call x1, Pallas kernels, body(): pl.pallas_call(kernel, name='loftq', out_shape=(jax.ShapeDtypeStruct((per...  211 us
    pallas_call x1, Pallas kernels, body(): pl.pallas_call(finish, name='finish', out_shape=tuple((jax.ShapeDtypeStru...  8.53 us

profile of v4, /device:TPU:1, one launch (start us, length us, event | category | flops | bytes accessed | tf_op | source)
XLA Modules:
  0.0 221.5 jit_solution(14489856688481435570)
XLA Ops:
  0.6 1.2 convert_element_type.3.codebook
  1.8 211.1 %loftq.1 = (bf16[96,53248]{1,0:T(8,128)(2,1)}, f32[96,832]{1,0:T(8,128)}, f32[64,3072]{1,0:T(8,128)}, f32[64,1664]{1,0:T(8,128)}) custom-call(bf16[3072,1664]{1,0:T(8,128)(2,1)} %weight.1, bf16[64,1664]{1,0:T(8,128)(2,1)} %bitcast.2, f32[16]{0:T(128)} %convert_element_type.3.codebook), custom_call_target="tpu_custom_call" | custom-call | tf_op jit(solution)/shard_map/loftq/pallas_call | solution.py:442
  212.9 8.5 %finish.1 = (bf16[96,53248]{1,0:T(8,128)(2,1)}, f32[96,832]{1,0:T(8,128)}, f32[64,3072]{1,0:T(8,128)}, f32[64,1664]{1,0:T(8,128)}) custom-call(bf16[96,53248]{1,0:T(8,128)(2,1)} %get-tuple-element.12.refs_0_, f32[96,832]{1,0:T(8,128)} %get-tuple-element.13.refs_1_, f32[64,3072]{1,0:T(8,128)} %get-tuple-element.14.refs_2_, f32[64,1664]{1,0:T(8,128)} %get-tuple-element.15.refs_3_), custom_call_target="tpu_custom_call" | custom-call | tf_op jit(solution)/shard_map/finish/pallas_call | solution.py:492
